TPU v7x, 32 devices: a whole 2x2x4 slice. The times are simulated.
32 devices in a mesh: groups: 2 (over x), ctx: 2 (over core), fsdp: 8 (over z, y).
Axes of the slice: x: 2, y: 2, z: 4, core: 2. Of those that a mesh axis runs over, the one named last changes fastest.
Arguments:
- hidden_in: bfloat16 [8192, 2048], P(('groups', 'ctx', 'fsdp')), parts along dimension 0, may hold values from -6 to 6
- qkv_weight: bfloat16 [2048, 4096], P(None, 'fsdp'), may hold values from -0.125 to 0.125
- ab_weight: bfloat16 [2048, 32], replicated, may hold values from -0.125 to 0.125
- conv_weight: float32 [4, 4096], replicated, may hold values from -3 to 3
- decay_rate: float32 [16], replicated, may hold values from 7.324219e-05 to 0.3
- dt_bias: float32 [16], replicated, may hold values from -3 to -1
- norm_gain: float32 [128], replicated, may hold values from 0.1 to 1.9
- previous_tail: bfloat16 [6, 4096], P('groups'), parts along dimension 0, may hold values from -6 to 6
- window_entry_state: float32 [32, 128, 128], P('groups'), parts along dimension 0, may hold values from -3 to 3
Outputs:
- head_out: bfloat16 [8192, 2048], P(('groups', 'ctx', 'fsdp')), parts along dimension 0
There are 2 independent parts, one for each index of `groups`. A program takes and returns all parts, laid end to end along the dimension named above; an argument that names none is the same for every part. Nothing has to cross between parts.
All inputs are finite; a program needn't handle non-finite values.
Results may differ from a plain program's by a relative error of at most 0.0065.
Values may be sent and summed in bfloat16 or wider, within the bound.
A program may use at most 320 MiB of HBM per device.

v0:
```python
import jax
import jax.numpy as jnp
from jax import lax
from jax.sharding import PartitionSpec as P

HK = 8
HV = 16
DK = 128
DV = 128
SPAN = 64
exact_product = lax.Precision.HIGHEST


def shifted(array, axis, by):
    peers = lax.axis_size(axis)
    pairs = [(i, i + by) for i in range(peers) if 0 <= i + by < peers]
    return lax.ppermute(array, axis, pairs)


def entering(part, axis, combine, identity):
    place = lax.axis_index(axis)
    gathered = jax.tree.map(lambda a: lax.all_gather(a, axis), part)
    state = jax.tree.map(lambda a, e: jnp.zeros_like(a) + jnp.asarray(e, a.dtype), part, identity)

    def one(hop, state):
        return combine(
            state, jax.tree.map(lambda a: lax.dynamic_index_in_dim(a, hop, 0, False), gathered)
        )

    return lax.fori_loop(0, place, one, state)


def unit_norm(vectors):
    return vectors * lax.rsqrt(jnp.sum(vectors * vectors, axis=-1, keepdims=True) + 1e-06)


def convolve(before, mixed_qkv, conv_weight):
    length = mixed_qkv.shape[0]
    padded = jnp.concatenate([before, mixed_qkv], axis=0).astype(jnp.float32)
    summed = jnp.zeros((length, mixed_qkv.shape[1]), jnp.float32)
    for offset in range(conv_weight.shape[0]):
        summed = summed + conv_weight[offset] * padded[offset : offset + length]
    return jax.nn.silu(summed)


def to_spans(tensor, span_len):
    length, head_count = (tensor.shape[0], tensor.shape[1])
    shaped = tensor.reshape((length // span_len, span_len, head_count) + tensor.shape[2:])
    return jnp.moveaxis(shaped, 2, 1)


def head_inputs(conv_out, gate_logits, decay_rate, dt_bias):
    length = conv_out.shape[0]
    queries = unit_norm(conv_out[:, : HK * DK].reshape(length, HK, DK)) * DK ** (-0.5)
    head_keys = unit_norm(conv_out[:, HK * DK : 2 * HK * DK].reshape(length, HK, DK))
    values = conv_out[:, 2 * HK * DK :].reshape(length, HV, DV)
    queries = jnp.repeat(queries, HV // HK, axis=1)
    head_keys = jnp.repeat(head_keys, HV // HK, axis=1)
    write_rate = jax.nn.sigmoid(gate_logits[:, HV:])
    logdecay = -decay_rate * jax.nn.softplus(gate_logits[:, :HV] + dt_bias)
    return [to_spans(item, SPAN) for item in (queries, head_keys, values, write_rate, logdecay)]


def lower_inverse(strict_part):
    span_len = strict_part.shape[-1]
    unit_span = jnp.eye(span_len, dtype=strict_part.dtype)
    inverse = unit_span - strict_part
    power = strict_part
    reach = 2
    while reach < span_len:
        power = jnp.einsum("...ij,...jk->...ik", power, power, precision=exact_product)
        inverse = inverse + jnp.einsum(
            "...ij,...jk->...ik", inverse, power, precision=exact_product
        )
        reach = reach * 2
    return inverse


def span_terms(queries, head_keys, values, write_rate, logdecay):
    span_len = logdecay.shape[-1]
    cumulative = jnp.cumsum(logdecay, axis=-1)
    row_index = lax.broadcasted_iota(jnp.int32, (span_len, span_len), 0)
    col_index = lax.broadcasted_iota(jnp.int32, (span_len, span_len), 1)
    lower_mask = row_index >= col_index
    gap_log = cumulative[..., :, None] - cumulative[..., None, :]
    factor = jnp.where(lower_mask, jnp.exp(jnp.where(lower_mask, gap_log, 0.0)), 0.0)
    strict = jnp.where(row_index > col_index, factor, 0.0)
    key_products = jnp.einsum("...ik,...jk->...ij", head_keys, head_keys, precision=exact_product)
    query_products = jnp.einsum("...ik,...jk->...ij", queries, head_keys, precision=exact_product)
    inverse = lower_inverse(write_rate[..., :, None] * key_products * strict)
    growth = jnp.exp(cumulative)
    right_sides = jnp.concatenate(
        [write_rate[..., None] * values, (write_rate * growth)[..., None] * head_keys], axis=-1
    )
    solved = jnp.einsum("...ij,...jc->...ic", inverse, right_sides, precision=exact_product)
    new_values = solved[..., : values.shape[-1]]
    key_weights = solved[..., values.shape[-1] :]
    scores = query_products * factor
    window_local_output = jnp.einsum(
        "...ij,...jv->...iv", scores, new_values, precision=exact_product
    )
    effective_query = growth[..., None] * queries - jnp.einsum(
        "...ij,...jk->...ik", scores, key_weights, precision=exact_product
    )
    span_end = cumulative[..., -1]
    tail_decay = jnp.exp(span_end[..., None] - cumulative)
    decayed_keys = head_keys * tail_decay[..., None]
    unit_key = jnp.eye(head_keys.shape[-1], dtype=logdecay.dtype)
    state_mapping = jnp.exp(span_end)[..., None, None] * unit_key - jnp.einsum(
        "...ck,...cj->...kj", decayed_keys, key_weights, precision=exact_product
    )
    shifted_state = jnp.einsum(
        "...ck,...cv->...kv", decayed_keys, new_values, precision=exact_product
    )
    return (effective_query, window_local_output, state_mapping, shifted_state)


def finish(result_rows, norm_gain):
    mean_square = jnp.mean(result_rows * result_rows, axis=-1, keepdims=True)
    normed = result_rows * lax.rsqrt(mean_square + 1e-06) * norm_gain
    normed = jnp.moveaxis(normed, 1, 2)
    return normed.reshape(
        normed.shape[0] * normed.shape[1], normed.shape[2] * normed.shape[3]
    ).astype(jnp.bfloat16)


def compose(former_piece, latter_piece):
    joined_map = jnp.einsum(
        "hkj,hjm->hkm", latter_piece[0], former_piece[0], precision=exact_product
    )
    combined_state = (
        jnp.einsum("zom,zmg->zog", latter_piece[0], former_piece[1], precision=exact_product)
        + latter_piece[1]
    )
    return (joined_map, combined_state)


def shards(
    hidden_in,
    qkv_weight,
    ab_weight,
    conv_weight,
    decay_rate,
    dt_bias,
    norm_gain,
    previous_tail,
    window_entry_state,
):
    mixed_qkv = jnp.dot(
        hidden_in,
        lax.all_gather(qkv_weight, "fsdp", axis=1, tiled=True),
        preferred_element_type=jnp.float32,
    ).astype(jnp.bfloat16)
    gate_logits = jnp.dot(hidden_in, ab_weight, preferred_element_type=jnp.float32)
    tail_rows = previous_tail.shape[0]
    received = shifted(mixed_qkv[mixed_qkv.shape[0] - tail_rows :], ("ctx", "fsdp"), 1)
    before = jnp.where(lax.axis_index(("ctx", "fsdp")) == 0, previous_tail, received)
    conv_out = convolve(before, mixed_qkv, conv_weight)
    spanned = head_inputs(conv_out, gate_logits, decay_rate, dt_bias)
    effective_query, window_local_output, state_mapping, shifted_state = span_terms(*spanned)
    unit_maps = jnp.broadcast_to(jnp.eye(DK, dtype=jnp.float32), (HV, DK, DK))
    empty_state = jnp.zeros((HV, DK, DV), jnp.float32)

    def advance(carried, items):
        carry_map, carried_over_state = carried
        per_step_query, per_step_local, per_step_mapping, step_offset = items
        adjusted_result = jnp.einsum(
            "hck,hkj->hcj", per_step_query, carry_map, precision=exact_product
        )
        layer_result = per_step_local + jnp.einsum(
            "gpi,gib->gpb", per_step_query, carried_over_state, precision=exact_product
        )
        carry_map = jnp.einsum("hkj,hjm->hkm", per_step_mapping, carry_map, precision=exact_product)
        carried_over_state = (
            jnp.einsum(
                "zom,zmg->zog", per_step_mapping, carried_over_state, precision=exact_product
            )
            + step_offset
        )
        return ((carry_map, carried_over_state), (adjusted_result, layer_result))

    own_pair, (adjusted_result, incomplete_output) = lax.scan(
        advance,
        (unit_maps, empty_state),
        (effective_query, window_local_output, state_mapping, shifted_state),
    )
    identity = (unit_maps, empty_state)
    leading_pair = entering((own_pair[0], own_pair[1]), ("ctx", "fsdp"), compose, identity)
    opening_state = (
        jnp.einsum("zom,zmg->zog", leading_pair[0], window_entry_state, precision=exact_product)
        + leading_pair[1]
    )
    result_rows = incomplete_output + jnp.einsum(
        "elfx,lxw->elfw", adjusted_result, opening_state, precision=exact_product
    )
    return finish(result_rows, norm_gain)


def solution(mesh):
    placed = (
        P(("groups", "ctx", "fsdp"), None),
        P(None, "fsdp"),
        P(),
        P(),
        P(),
        P(),
        P(),
        P("groups", None),
        P("groups", None, None),
    )
    return jax.shard_map(
        shards,
        mesh=mesh,
        in_specs=placed,
        out_specs=P(("groups", "ctx", "fsdp"), None),
        check_vma=False,
    )
```

profile of v0, /device:TPU:31, one launch (start us, length us, event | category | flops | bytes accessed | tf_op | source)
XLA Modules:
  0.0 710.3 jit_solution(9324896033051884628)
XLA Ops:
  9.7 225.8 %all-gather.6.cloned.1.call-done = bf16[2048,4096]{1,0:T(8,128)(2,1)} async-done(((bf16[2048,512]{1,0:T(8,128)(2,1)}), bf16[2048,4096]{1,0:T(8,128)(2,1)}) %all-gather.6.cloned.1.call-update) | async-done | bytes 16777232 | tf_op jit(solution)/shard_map/all_gather | solution.py:151
  235.5 8.4 %convolution_convert_fusion = bf16[256,4096]{1,0:T(8,128)(2,1)S(1)} fusion(bf16[256,2048]{1,0:T(8,128)(2,1)S(1)} %copy-done, bf16[2048,4096]{1,0:T(8,128)(2,1)} %all-gather.6.cloned.1.call-done), kind=kOutput, calls=%fused_computation.35 | convolution fusion | flops 4296015872 | bytes 19922944 | tf_op jit(solution)/shard_map/dot_general | solution.py:149
  246.5 3.0 collective-permute-done
  250.9 2.8 divide_multiply_fusion
  257.3 3.5 fusion.45
  260.8 3.6 select_multiply_fusion
  266.6 2.7 fusion.88
  269.4 2.5 subtract_add_fusion
  278.7 2.5 fusion.90
  283.4 2.4 convolution_add_fusion.3
  289.3 4.5 fusion.34
  293.8 3.6 fusion.47
  297.4 3.9 fusion.40
  301.4 8.9 %fusion.46 = f32[4,16,128,128]{3,2,1,0:T(8,128)} fusion(f32[4,16,64,256]{3,2,1,0:T(8,128)S(1)} %fusion.34, f32[4,64,16,128]{3,1,0,2:T(8,128)S(1)} %bitcast.166, f32[4,16,64]{2,1,0:T(8,128)S(1)} %get-tuple-element.163), kind=kOutput, calls=%fused_computation.68 | convolution fusion | flops 805830656 | bytes 8421376 | tf_op jit(solution)/shard_map/...ck,...cv->...kv/dot_general | solution.py:112
  310.2 9.7 %multiply_subtract_fusion = f32[4,16,128,128]{3,2,1,0:T(8,128)} fusion(f32[128,128]{1,0:T(8,128)S(1)} %fusion.76, f32[4,16]{1,0:T(4,128)S(1)} %exp.36, f32[4,16,64,256]{3,2,1,0:T(8,128)S(1)} %fusion.34, f32[4,64,16,128]{3,1,0,2:T(8,128)S(1)} %bitcast.167, f32[4,16,64]{2,1,0:T(8,128)S(1)} %get-tuple-element.163), kind=kOutput, calls=%fused_computation.48 | convolution fusion | flops 807927808 | bytes 8488960 | tf_op jit(solution)/shard_map/...ck,...cj->...kj/dot_general | solution.py:109
  320.0 39.9 %while.30 = (s32[]{:T(128)}, f32[16,128,128]{2,1,0:T(8,128)S(1)}, f32[16,128,128]{2,1,0:T(8,128)S(1)}, f32[4,16,64,128]{3,2,0,1:T(8,128)}, f32[4,16,64,128]{3,2,...) while((s32[]{:T(128)}, f32[16,128,128]{2,1,0:T(8,128)S(1)}, ...), condition=%wide.region_4.5_spmd.clone, body=%wide.region_3.4_spmd.clone.sunk | while | flops 1208877056 | bytes 41423032 | solution.py:182
  324.7 2.9 fusion.157
  334.6 2.9 fusion.157
  344.6 2.9 fusion.157
  354.6 2.9 fusion.157
  361.7 126.7 %all-gather.8.cloned.1.call-done = f32[256,128,128]{2,1,0:T(8,128)} async-done(((f32[16,128,128]{2,1,0:T(8,128)}), f32[256,128,128]{2,1,0:T(8,128)}) %all-gather.8.cloned.1.call-update) | async-done | bytes 16777232 | tf_op jit(solution)/shard_map/all_gather | solution.py:22
  488.4 127.3 %all-gather.10.cloned.1.call-done = f32[256,128,128]{2,1,0:T(8,128)} async-done(((f32[16,128,128]{2,1,0:T(8,128)}), f32[256,128,128]{2,1,0:T(8,128)}) %all-gather.10.cloned.1.call-update) | async-done | bytes 16777232 | tf_op jit(solution)/shard_map/all_gather | solution.py:22
  615.9 80.2 %while.29 = (s32[]{:T(128)}, f32[16,128,128]{2,1,0:T(8,128)S(1)}, f32[16,128,128]{2,1,0:T(8,128)S(1)}, s32[]{:T(128)}, f32[16,16,128,128]{3,2,1,0:T(8,128)}, /*i...) while((s32[]{:T(128)}, f32[16,128,128]{2,1,0:T(8,128)S(1)}, ...), condition=%wide.region_6.7_spmd, body=%wide.region_5.6_spmd.sunk | while | flops 805568512 | bytes 11535499 | solution.py:30
  616.1 2.8 convolution_add_fusion.8
  618.9 2.4 fusion.146
  621.6 2.7 convolution_add_fusion.8
  624.3 2.4 fusion.146
  626.9 2.7 convolution_add_fusion.8
  632.2 2.7 convolution_add_fusion.8
  634.9 2.4 fusion.146
  637.5 2.7 convolution_add_fusion.8
  642.8 2.7 convolution_add_fusion.8
  645.5 2.4 fusion.146
  648.1 2.7 convolution_add_fusion.8
  653.5 2.7 convolution_add_fusion.8
  658.8 2.8 convolution_add_fusion.8
  661.6 2.4 fusion.146
  664.2 2.7 convolution_add_fusion.8
  669.5 2.7 convolution_add_fusion.8
  672.2 2.4 fusion.146
  674.9 2.7 convolution_add_fusion.8
  677.6 2.4 fusion.146
  680.2 2.7 convolution_add_fusion.8
  682.9 2.4 fusion.146
  685.5 2.7 convolution_add_fusion.8
  688.2 2.4 fusion.146
  690.8 2.7 convolution_add_fusion.8
  698.4 2.5 multiply_reduce_fusion
  (158 shorter events, 76.6 us)
Async XLA Ops:
  6.5 1.2 copy-start
  6.5 0.8 copy-start.15
  6.5 1.2 copy-start.9
  6.5 1.7 copy-start.13
  6.5 3.1 copy-start.10
  6.5 228.9 %all-gather.6.cloned.1.call-start = ((), (), s32[]{:S(2)}) async-start(), calls=%async_computation | async-start | bytes 18874368 | tf_op jit(solution)/shard_map/all_gather | solution.py:151
  7.3 481.1 %all-gather.8.cloned.1.call-start = ((), (), s32[]{:S(2)}) async-start(), calls=%async_computation.1 | async-start | bytes 17825792 | tf_op jit(solution)/shard_map/all_gather | solution.py:22
  9.7 239.8 %copy-start.11 = (bf16[3,4096]{1,0:T(4,128)(2,1)S(1)}, bf16[3,4096]{1,0:T(4,128)(2,1)}, u32[]{:S(2)}) copy-start(bf16[3,4096]{1,0:T(4,128)(2,1)} %param.20) | copy-start | bytes 73732
  244.5 5.0 collective-permute-start
  257.3 3.5 copy-start.12
  320.0 1.6 copy-start.5
  320.1 3.4 copy-start.2
  330.0 1.6 copy-start.5
  330.1 3.4 copy-start.2
  340.0 1.6 copy-start.5
  340.1 3.4 copy-start.2
  350.0 1.6 copy-start.5
  350.1 3.4 copy-start.2
  359.9 1.0 copy-start.3
  360.0 1.3 copy-start.4
  360.9 254.8 %all-gather.10.cloned.1.call-start = ((), (), s32[]{:S(2)}) async-start(), calls=%async_computation.2 | async-start | bytes 17825792 | tf_op jit(solution)/shard_map/all_gather | solution.py:22
  615.9 80.2 %copy-start.8 = (f32[16,128,128]{2,1,0:T(8,128)S(1)}, f32[16,128,128]{2,1,0:T(8,128)}, u32[]{:S(2)}) copy-start(f32[16,128,128]{2,1,0:T(8,128)} %param.21) | copy-start | bytes 3145732
  696.2 1.6 copy-start.6
  696.2 2.2 copy-start.7
  698.4 2.5 copy-start.14
  701.0 2.7 copy-start.1
Sparse Core Ops, SparseCore 0:
  9.4 226.0 all-gather.5
  361.1 127.2 all-gather.7
  490.6 125.0 all-gather.9
where the time goes:
time: 716 us; the launch traced here: 710 us
  waiting for transfers between devices  484 us (68%)
  matrix products  184 us (26%)
  local copies, waits for them, and re-layouts  16.5 us (2%)
  between operations  13.8 us (2%)
  other arithmetic  9.23 us (1%)
    all_gather x2, waiting for transfers between devices, entering(): gathered = jax.tree.map(lambda a: lax.all_gather(a, axis), part)  254 us
    all_gather x1, waiting for transfers between devices, shards(): lax.all_gather(qkv_weight, 'fsdp', axis=1, tiled=True)  226 us
    dot_general x15, matrix products, compose(): jnp.einsum('zom,zmg->zog', latter_piece[0], former_piece[1], precision=ex...  40.7 us
    dot_general x15, matrix products, compose(): jnp.einsum('hkj,hjm->hkm', latter_piece[0], former_piece[0], precision=ex...  36.3 us
  transfers between devices with their start and end apart: 4, of which 4 were waited for; matrix products, arithmetic and copies ran while one was open for 0% of the time, Pallas kernels for 0%

commit v1 on v0

--- a/solution.py
+++ b/solution.py
@@ -1,3 +1,4 @@
+import functools
 import jax
 import jax.numpy as jnp
 from jax import lax
@@ -9,6 +10,28 @@
 DV = 128
 SPAN = 64
 exact_product = lax.Precision.HIGHEST
+
+
+def _recover_edge(shard_in, row_dim):
+    z_new, high, h_now = (lax.axis_size("fsdp"), lax.axis_index("fsdp"), shard_in.shape[row_dim])
+    tall, main = (shard_in, 1)
+    while main < z_new:
+        tall = jnp.concatenate(
+            [
+                tall,
+                lax.ppermute(
+                    tall,
+                    axis_name="fsdp",
+                    perm=tuple(((nth, (nth - main) % z_new) for nth in range(z_new))),
+                ),
+            ],
+            axis=row_dim,
+        )
+        main = 2 * main
+    return jnp.roll(tall, shift=high * h_now, axis=row_dim)
+
+
+take_object_in = functools.partial(_recover_edge, row_dim=1)
 
 
 def shifted(array, axis, by):
@@ -147,9 +170,7 @@
     window_entry_state,
 ):
     mixed_qkv = jnp.dot(
-        hidden_in,
-        lax.all_gather(qkv_weight, "fsdp", axis=1, tiled=True),
-        preferred_element_type=jnp.float32,
+        hidden_in, take_object_in(qkv_weight), preferred_element_type=jnp.float32
     ).astype(jnp.bfloat16)
     gate_logits = jnp.dot(hidden_in, ab_weight, preferred_element_type=jnp.float32)
     tail_rows = previous_tail.shape[0]

time: 716 us -> 1020 us (1.42)
  waiting for transfers between devices: 484 us -> 750 us
  local copies, waits for them, and re-layouts: 16.5 us -> 41.2 us
    ppermute x0 -> x3, waiting for transfers between devices: none -> 493 us  [_recover_edge(): lax.ppermute(tall, axis_name='fsdp', perm=tuple(((nth, (nth - main) % z_n...]
    all_gather x1 -> x0, waiting for transfers between devices: 226 us -> none  [shards(): lax.all_gather(qkv_weight, 'fsdp', axis=1, tiled=True)]
    unnamed x34 -> x51, local copies, waits for them, and re-layouts: 5.13 us -> 27.1 us
  transfers between devices with their start and end apart: 4 -> 6, of which waited for: 4 -> 6; matrix products, arithmetic and copies ran while one was open for 0% -> 1% of each run, Pallas kernels for 0% -> 0%
where the time goes in v1:
time: 1020 us
  waiting for transfers between devices  750 us (74%)
  matrix products  192 us (19%)
  local copies, waits for them, and re-layouts  41.2 us (4%)
  other arithmetic  16.9 us (2%)
  between operations  14.2 us (1%)
    ppermute x3, waiting for transfers between devices, _recover_edge(): lax.ppermute(tall, axis_name='fsdp', perm=tuple(((nth, (nth - main) % z_n...  493 us
    all_gather x2, waiting for transfers between devices, entering(): gathered = jax.tree.map(lambda a: lax.all_gather(a, axis), part)  253 us
    dot_general x15, matrix products, compose(): jnp.einsum('zom,zmg->zog', latter_piece[0], former_piece[1], precision=ex...  41.3 us
    dot_general x15, matrix products, compose(): jnp.einsum('hkj,hjm->hkm', latter_piece[0], former_piece[0], precision=ex...  35.7 us
    unnamed x51, local copies, waits for them, and re-layouts  27.1 us
  transfers between devices with their start and end apart: 6, of which 6 were waited for; matrix products, arithmetic and copies ran while one was open for 1% of the time, Pallas kernels for 0%

profile of v1, /device:TPU:31, one launch (start us, length us, event | category | flops | bytes accessed | tf_op | source)
XLA Modules:
  0.0 1016.8 jit_solution(14191765541959267704)
XLA Ops:
  6.8 49.2 %collective-permute-done = bf16[2048,512]{1,0:T(8,128)(2,1)S(1)} collective-permute-done((bf16[2048,512]{1,0:T(8,128)(2,1)}, bf16[2048,512]{1,0:T(8,128)(2,1)S(1)}, u32[]{:S(2)}, u32[]{:S(2)}) %collective-permute-start) | collective-permute-done | bytes 2097184 | tf_op jit(solution)/shard_map/ppermute | solution.py:22
  56.0 3.0 pad_maximum_fusion.1
  59.1 92.3 %collective-permute-done.1 = bf16[2048,1024]{1,0:T(8,128)(2,1)S(1)} collective-permute-done((bf16[2048,1024]{1,0:T(8,128)(2,1)S(1)}, bf16[2048,1024]{1,0:T(8,128)(2,1)S(1)}, u32[]{:S(2)}, u32[]{:S(2)}) %collective-permute-start.1) | collective-permute-done | bytes 4194336 | tf_op jit(solution)/shard_map/ppermute | solution.py:22
  151.4 4.5 pad_maximum_fusion
  165.5 351.9 %collective-permute-done.2 = bf16[2048,2048]{1,0:T(8,128)(2,1)} collective-permute-done((bf16[2048,2048]{1,0:T(8,128)(2,1)}, bf16[2048,2048]{1,0:T(8,128)(2,1)}, u32[]{:S(2)}, u32[]{:S(2)}) %collective-permute-start.2) | collective-permute-done | bytes 8388640 | tf_op jit(solution)/shard_map/ppermute | solution.py:22
  517.4 8.3 constant_dynamic-update-slice_fusion.4
  525.7 3.2 constant_dynamic-update-slice_fusion.3
  532.7 8.4 constant_dynamic-update-slice_fusion
  541.1 8.4 fusion.36
  552.1 3.0 collective-permute-done.3
  556.5 3.0 divide_multiply_fusion
  562.7 3.5 fusion.53
  566.3 3.7 select_multiply_fusion
  574.7 2.6 subtract_add_fusion
  584.3 2.6 fusion.99
  595.6 4.7 fusion.42
  600.4 3.6 fusion.55
  604.0 3.9 fusion.48
  607.9 8.9 fusion.54
  616.8 9.4 multiply_subtract_fusion
  626.4 39.8 %while.30 = (s32[]{:T(128)}, f32[16,128,128]{2,1,0:T(8,128)S(1)}, f32[16,128,128]{2,1,0:T(8,128)S(1)}, f32[4,16,64,128]{3,2,0,1:T(8,128)}, f32[4,16,64,128]{3,2,...) while((s32[]{:T(128)}, f32[16,128,128]{2,1,0:T(8,128)S(1)}, ...), condition=%wide.region_4.5_spmd.clone, body=%wide.region_3.4_spmd.clone.sunk | while | flops 1208877056 | bytes 33033364 | solution.py:203
  626.5 3.3 fusion.165
  632.2 2.9 fusion.164
  636.4 3.3 fusion.165
  642.2 2.9 fusion.164
  646.4 3.3 fusion.165
  652.1 2.9 fusion.164
  656.3 3.2 fusion.165
  662.1 2.9 fusion.164
  667.9 125.7 %all-gather.5.cloned.1.call-done = f32[256,128,128]{2,1,0:T(8,128)} async-done(((f32[16,128,128]{2,1,0:T(8,128)}), f32[256,128,128]{2,1,0:T(8,128)}) %all-gather.5.cloned.1.call-update) | async-done | bytes 16777232 | tf_op jit(solution)/shard_map/all_gather | solution.py:45
  793.7 127.3 %all-gather.7.cloned.1.call-done = f32[256,128,128]{2,1,0:T(8,128)} async-done(((f32[16,128,128]{2,1,0:T(8,128)}), f32[256,128,128]{2,1,0:T(8,128)}) %all-gather.7.cloned.1.call-update) | async-done | bytes 16777232 | tf_op jit(solution)/shard_map/all_gather | solution.py:45
  921.2 80.2 %while.29 = (s32[]{:T(128)}, f32[16,128,128]{2,1,0:T(8,128)S(1)}, f32[16,128,128]{2,1,0:T(8,128)S(1)}, s32[]{:T(128)}, f32[16,16,128,128]{3,2,1,0:T(8,128)}, /*i...) while((s32[]{:T(128)}, f32[16,128,128]{2,1,0:T(8,128)S(1)}, ...), condition=%wide.region_6.7_spmd, body=%wide.region_5.6_spmd.sunk | while | flops 805568512 | bytes 11535491 | solution.py:53
  921.3 2.8 convolution_add_fusion.8
  926.7 2.7 convolution_add_fusion.8
  932.0 2.7 convolution_add_fusion.8
  937.3 2.7 convolution_add_fusion.8
  942.6 2.7 convolution_add_fusion.8
  947.9 2.7 convolution_add_fusion.8
  953.2 2.7 convolution_add_fusion.8
  958.6 2.8 convolution_add_fusion.8
  963.9 2.8 convolution_add_fusion.8
  969.3 2.7 convolution_add_fusion.8
  974.6 2.7 convolution_add_fusion.8
  979.9 2.7 convolution_add_fusion.8
  985.3 2.8 convolution_add_fusion.8
  990.6 2.7 convolution_add_fusion.8
  995.9 2.7 convolution_add_fusion.8
  1002.9 4.0 multiply_reduce_fusion
  (173 shorter events, 100.0 us)
Async XLA Ops:
  6.5 149.3 %copy-start = (bf16[256,2048]{1,0:T(8,128)(2,1)S(1)}, bf16[256,2048]{1,0:T(8,128)(2,1)}, u32[]{:S(2)}) copy-start(bf16[256,2048]{1,0:T(8,128)(2,1)} %param.13) | copy-start | bytes 3145732
  6.5 144.8 %copy-start.7 = (bf16[2048,512]{1,0:T(8,128)(2,1)S(1)}, bf16[2048,512]{1,0:T(8,128)(2,1)}, u32[]{:S(2)}) copy-start(bf16[2048,512]{1,0:T(8,128)(2,1)} %param.14) | copy-start | bytes 6291460
  6.5 787.1 %all-gather.5.cloned.1.call-start = ((), (), s32[]{:S(2)}) async-start(), calls=%async_computation | async-start | bytes 17825792 | tf_op jit(solution)/shard_map/all_gather | solution.py:45
  6.5 49.4 %collective-permute-start = (bf16[2048,512]{1,0:T(8,128)(2,1)}, bf16[2048,512]{1,0:T(8,128)(2,1)S(1)}, u32[]{:S(2)}, u32[]{:S(2)}) collective-permute-start(bf16[2048,512]{1,0:T(8,128)(2,1)} %param.14), channel_id=1, source_target_pairs={{0,7},{1,0},{2,1},{3,2},{4,3},{5,4},{6,5},{7,6},{8,15},{9,8},{10,9... | collective-permute-start | bytes 6291464 | tf_op jit(solution)/shard_map/ppermute | solution.py:22
  55.9 95.4 %copy-start.8 = (bf16[2048,512]{1,0:T(8,128)(2,1)}, bf16[2048,512]{1,0:T(8,128)(2,1)S(1)}, u32[]{:S(2)}) copy-start(bf16[2048,512]{1,0:T(8,128)(2,1)S(1)} %collective-permute-done) | copy-start | bytes 6291460
  58.9 96.9 %copy-start.19 = (f32[16]{0:T(128)S(1)}, f32[16]{0:T(128)}, u32[]{:S(2)}) copy-start(f32[16]{0:T(128)} %param.17) | copy-start | bytes 196
  59.0 96.9 %copy-start.13 = (bf16[2048,32]{0,1:T(8,128)(2,1)S(1)}, bf16[2048,32]{0,1:T(8,128)(2,1)}, u32[]{:S(2)}) copy-start(bf16[2048,32]{0,1:T(8,128)(2,1)} %param.15) | copy-start | bytes 393220
  59.0 97.3 %copy-start.17 = (f32[16]{0:T(128)S(1)}, f32[16]{0:T(128)}, u32[]{:S(2)}) copy-start(f32[16]{0:T(128)} %param.18) | copy-start | bytes 196
  59.0 92.4 %collective-permute-start.1 = (bf16[2048,1024]{1,0:T(8,128)(2,1)S(1)}, bf16[2048,1024]{1,0:T(8,128)(2,1)S(1)}, u32[]{:S(2)}, u32[]{:S(2)}) collective-permute-start(bf16[2048,1024]{1,0:T(8,128)(2,1)S(1)} %pad_maximum_fusion.1), channel_id=1, source_target_pairs={{0,6},{1,7},{2,0},{3,1},{4,2},{5,3},{6,4},{7,5},{8,14},{9,15},{10,... | collective-permute-start | bytes 12582920 | tf_op jit(solution)/shard_map/ppermute | solution.py:22
  151.4 4.5 copy-start.5
  155.8 361.6 %collective-permute-start.2 = (bf16[2048,2048]{1,0:T(8,128)(2,1)}, bf16[2048,2048]{1,0:T(8,128)(2,1)}, u32[]{:S(2)}, u32[]{:S(2)}) collective-permute-start(bf16[2048,2048]{1,0:T(8,128)(2,1)} %pad_maximum_fusion), channel_id=1, source_target_pairs={{0,4},{1,5},{2,6},{3,7},{4,0},{5,1},{6,2},{7,3},{8,12},{9,13},{10,... | collective-permute-start | bytes 25165832 | tf_op jit(solution)/shard_map/ppermute | solution.py:22
  157.8 1.5 copy-start.14
  157.8 2.4 copy-start.9
  160.2 2.9 copy-start.6
  525.7 3.2 copy-start.10
  541.1 14.0 %copy-start.15 = (bf16[3,4096]{1,0:T(4,128)(2,1)S(1)}, bf16[3,4096]{1,0:T(4,128)(2,1)}, u32[]{:S(2)}) copy-start(bf16[3,4096]{1,0:T(4,128)(2,1)} %param.20) | copy-start | bytes 73732
  550.2 5.0 collective-permute-start.3
  562.7 3.5 copy-start.16
  626.4 3.4 copy-start.2
  636.3 3.4 copy-start.2
  646.3 3.4 copy-start.2
  656.2 3.3 copy-start.2
  666.2 1.0 copy-start.3
  666.2 1.3 copy-start.4
  667.2 253.8 %all-gather.7.cloned.1.call-start = ((), (), s32[]{:S(2)}) async-start(), calls=%async_computation.1 | async-start | bytes 17825792 | tf_op jit(solution)/shard_map/all_gather | solution.py:45
  921.2 80.2 %copy-start.12 = (f32[16,128,128]{2,1,0:T(8,128)S(1)}, f32[16,128,128]{2,1,0:T(8,128)}, u32[]{:S(2)}) copy-start(f32[16,128,128]{2,1,0:T(8,128)} %param.21) | copy-start | bytes 3145732
  1001.3 1.6 copy-start.11
  1002.9 4.1 copy-start.18
  1007.0 2.7 copy-start.1
Sparse Core Ops, SparseCore 0:
  667.3 126.3 all-gather.4
  795.9 125.0 all-gather.6
